TPU v7x, 32 devices: a whole 2x2x4 slice. The times are simulated.
32 devices in a mesh: groups: 2 (over y), expert: 16 (over z, x, core).
Axes of the slice: x: 2, y: 2, z: 4, core: 2. Of those that a mesh axis runs over, the one named last changes fastest.
Arguments:
- output_gradient: bfloat16 [4096, 3584], P(('groups', 'expert')), parts along dimension 0, may hold values from -0.59765625 to 0.59765625
- activations: bfloat16 [4096, 3584], P(('groups', 'expert')), parts along dimension 0, may hold values from -1.5 to 1.5
- scores: float32 [4096, 8], P(('groups', 'expert')), parts along dimension 0, may hold values from 0.02 to 0.98
- chosen_expert_index: int32 [4096, 8], P(('groups', 'expert')), parts along dimension 0, may hold values from 0 to 15, all different within a row; in each aligned block of 128 rows (0 to 127, 128 to 255, ...) at most 80 rows name the same one
- frozen_down_weight: bfloat16 [16, 1024, 3584], P('expert'), may hold values from -0.1875 to 0.1875
- adapter_first: bfloat16 [16, 1024, 32], P('expert'), may hold values from -0.1875 to 0.1875
- adapter_second: bfloat16 [16, 32, 3584], P('expert'), may hold values from -1 to 1
- stored_hidden_rows: bfloat16 [32, 1280, 1024], P(('groups', 'expert')), parts along dimension 0, may hold values from -6 to 6
Outputs:
- chosen_score_gradient: float32 [4096, 8], P(('groups', 'expert')), parts along dimension 0
- adapter_first_gradient: float32 [32, 1024, 32], P(('groups', 'expert')), parts along dimension 0
- adapter_second_gradient: float32 [32, 32, 3584], P(('groups', 'expert')), parts along dimension 0
- router_weight_gradient: float32 [32, 3584], P(('groups', 'expert')), parts along dimension 0
There are 2 independent parts, one for each index of `groups`. A program takes and returns all parts, laid end to end along the dimension named above; an argument that names none is the same for every part. Nothing has to cross between parts.
Inputs may be any that keep to these rules, and one draw needn't show every extreme that they name: `chosen_expert_index`: each row names 8 different experts. In the rows of one device no expert is named by more than 80 rows, a bound that some block reaches.
All inputs are finite; a program needn't handle non-finite values.
Results may differ from a plain program's by a relative error of at most 0.005.
Values may be sent and summed in bfloat16 or wider, within the bound.
A program may use at most 192 MiB of HBM per device.

v0:
```python
import jax
import jax.numpy as jnp
from jax import lax
from jax.sharding import PartitionSpec as P

adapter_scale = 2.0


def recompute_every_expert(hidden_activation, lowrank_hidden, expert_down_matrix, second_factor):
    return jnp.dot(
        hidden_activation, expert_down_matrix, preferred_element_type=jnp.float32
    ) + adapter_scale * jnp.dot(lowrank_hidden, second_factor, preferred_element_type=jnp.float32)


def per_device(
    output_gradient,
    activations,
    scores,
    chosen_expert_index,
    frozen_down_weight,
    adapter_first,
    adapter_second,
    stored_hidden_rows,
):
    devices = lax.axis_size("expert")
    exp_dev = frozen_down_weight.shape[0]
    slot_rows = stored_hidden_rows.shape[1]
    capacity = slot_rows // devices
    experts = exp_dev * devices
    tokens_dev = output_gradient.shape[0]
    chosen = scores.shape[1]
    features = output_gradient.shape[1]
    score_sum = jnp.sum(scores, axis=1, keepdims=True)
    weights = scores / score_sum
    slot_weight = weights.astype(jnp.bfloat16)
    flat_ids = chosen_expert_index.reshape(-1)
    one_hot = (flat_ids[:, None] == jnp.arange(experts, dtype=jnp.int32)[None, :]).astype(jnp.int32)
    slot_index = jnp.sum((jnp.cumsum(one_hot, axis=0) - 1) * one_hot, axis=1)
    position = flat_ids * capacity + slot_index
    repeated = jnp.repeat(output_gradient, chosen, axis=0)
    send_rows = jnp.zeros((experts * capacity, features), jnp.bfloat16).at[position].set(repeated)
    send_scale = (
        jnp.zeros((experts * capacity,), jnp.bfloat16).at[position].set(slot_weight.reshape(-1))
    )
    send_rows = send_rows.reshape(devices, exp_dev, capacity, features)
    send_scale = send_scale.reshape(devices, exp_dev, capacity)
    expert_number = 0
    hidden_activation = stored_hidden_rows[expert_number]
    lowrank_hidden = jnp.dot(
        hidden_activation, adapter_first[expert_number], preferred_element_type=jnp.float32
    ).astype(jnp.bfloat16)
    expert_output = recompute_every_expert(
        hidden_activation,
        lowrank_hidden,
        frozen_down_weight[expert_number],
        adapter_second[expert_number],
    )
    lows = [lowrank_hidden]
    outputs = [expert_output]
    recv_rows, recv_scale = (
        lax.all_to_all(send_rows, "expert", split_axis=0, concat_axis=0, tiled=True),
        lax.all_to_all(send_scale, "expert", split_axis=0, concat_axis=0, tiled=True),
    )
    expert_number = 0
    slot_grad = recv_rows[:, expert_number].reshape(slot_rows, features)
    slot_scale = recv_scale[:, expert_number].reshape(slot_rows)
    slot_inner_product = jnp.sum(slot_grad.astype(jnp.float32) * outputs[expert_number], axis=1)
    scaled_output_gradient = (
        slot_scale.astype(jnp.float32)[:, None] * slot_grad.astype(jnp.float32)
    ).astype(jnp.bfloat16)
    backward_lowrank = lax.dot_general(
        scaled_output_gradient,
        adapter_second[expert_number],
        (((1,), (1,)), ((), ())),
        preferred_element_type=jnp.float32,
    ).astype(jnp.bfloat16)
    first_factor_gradient = adapter_scale * lax.dot_general(
        stored_hidden_rows[expert_number],
        backward_lowrank,
        (((0,), (0,)), ((), ())),
        preferred_element_type=jnp.float32,
    )
    second_factor_gradient = adapter_scale * lax.dot_general(
        lows[expert_number],
        scaled_output_gradient,
        (((0,), (0,)), ((), ())),
        preferred_element_type=jnp.float32,
    )
    dots = [slot_inner_product.reshape(devices, capacity)]
    grads_a = [first_factor_gradient]
    grads_b = [second_factor_gradient]
    dot_table = jnp.stack(dots, axis=1)
    returned = lax.all_to_all(dot_table, "expert", split_axis=0, concat_axis=0, tiled=True)
    weight_grad = returned.reshape(experts * capacity)[position].reshape(tokens_dev, chosen)
    mixed = jnp.sum(weights * weight_grad, axis=1, keepdims=True)
    chosen_score_gradient = (weight_grad - mixed) / score_sum
    logit_grad = (chosen_score_gradient * scores * (1.0 - scores)).astype(jnp.bfloat16)
    matches = chosen_expert_index[None, :, :] == jnp.arange(experts, dtype=jnp.int32)[:, None, None]
    router_matrix = jnp.sum(
        jnp.where(matches, logit_grad.astype(jnp.float32)[None, :, :], 0.0), axis=2
    ).astype(jnp.bfloat16)
    router_weight_gradient = lax.psum_scatter(
        jnp.dot(router_matrix, activations, preferred_element_type=jnp.float32),
        "expert",
        scatter_dimension=0,
        tiled=True,
    )
    return (
        chosen_score_gradient,
        jnp.stack(grads_a, axis=0),
        jnp.stack(grads_b, axis=0),
        router_weight_gradient,
    )


def solution(mesh):
    placed = (
        P(("groups", "expert"), None),
        P(("groups", "expert"), None),
        P(("groups", "expert"), None),
        P(("groups", "expert"), None),
        P("expert", None, None),
        P("expert", None, None),
        P("expert", None, None),
        P(("groups", "expert"), None, None),
    )
    return jax.shard_map(
        per_device,
        mesh=mesh,
        in_specs=placed,
        out_specs=(
            P(("groups", "expert"), None),
            P(("groups", "expert"), None, None),
            P(("groups", "expert"), None, None),
            P(("groups", "expert"), None),
        ),
        check_vma=False,
    )
```

profile of v0, /device:TPU:0, one launch (start us, length us, event | category | flops | bytes accessed | tf_op | source)
XLA Modules:
  0.0 382.3 jit_solution(1614959234540488646)
XLA Ops:
  7.2 0.0 copy-start
  7.2 0.9 copy.63
  8.1 0.1 eq.42
  8.2 0.1 eq.38
  8.3 0.7 broadcast_multiply_fusion
  9.0 4.5 %reduce-window.6 = s32[16,8,128]{2,1,0:T(8,128)S(1)} reduce-window(s32[16,8,128]{2,1,0:T(8,128)S(1)} %fusion.31, s32[]{:T(128)} %constant.10.clone.1), window={size=1x1x128 pad=0_0x0_0x127_0}, to_apply=%region_0.0 | reduce-window | flops 2080768 | bytes 131076 | tf_op jit(solution)/shard_map/reduce-window
  13.5 0.1 slice.10
  13.6 0.1 copy.65
  13.8 0.1 copy.66
  13.8 0.1 add_add_fusion
  13.9 0.1 copy.62
  14.0 0.1 mul.67
  14.2 15.7 %scatter_custom_fusion = bf16[1280,3584]{1,0:T(8,128)(2,1)} fusion(s32[1024]{0:T(1024)S(1)} %bitcast.71, bf16[]{:T(256)} %constant.8.clone.1, bf16[128,3584]{1,0:T(8,128)(2,1)} %param.8), kind=kCustom, calls=%fused_computation.11 | custom fusion | bytes 10092546 | tf_op jit(solution)/shard_map/scatter | solution.py:41
  29.9 0.0 copy-start.2
  29.9 7.5 %all-to-all-start = ((bf16[16,1,80,3584]{3,2,1,0:T(8,128)(2,1)}), bf16[16,1,80,3584]{3,2,1,0:T(8,128)(2,1)}, u32[]{:S(2)}, u32[]{:S(2)}) async-start(bf16[16,1,80,3584]{3,2,1,0:T(8,128)(2,1)} %bitcast.65), calls=%async_computation | async-start | bytes 18350080 | tf_op jit(solution)/shard_map/all_to_all | solution.py:61
  37.4 0.0 copy-done
  37.5 0.0 copy-done.2
  37.5 0.9 fusion.16
  38.3 0.0 copy-start.1
  38.4 15.5 %fusion.3 = f32[1280,3584]{1,0:T(8,128)} fusion(bf16[1,1024,3584]{2,1,0:T(8,128)(2,1)} %param.12, bf16[1,1280,1024]{2,1,0:T(8,128)(2,1)S(1)} %copy-done), kind=kOutput, calls=%fused_computation.9 | convolution fusion | flops 9395240960 | bytes 28311552 | tf_op jit(solution)/shard_map/dot_general | solution.py:10
  53.9 148.0 %all-to-all-done = bf16[16,1,80,3584]{3,2,1,0:T(8,128)(2,1)} async-done(((bf16[16,1,80,3584]{3,2,1,0:T(8,128)(2,1)}), bf16[16,1,80,3584]{3,2,1,0:T(8,128)(2,1)}, u32[]{:S(2)}, u32[]{:S(2)}) %all-to-all-start) | async-done | bytes 9175072 | tf_op jit(solution)/shard_map/all_to_all | solution.py:61
  201.8 0.0 copy-done.1
  201.8 0.0 copy-start.4
  201.8 0.0 copy-start.5
  201.8 0.0 copy-start.3
  201.9 10.6 %fusion.10 = f32[1280]{0:T(1024)S(1)} fusion(f32[1280,3584]{1,0:T(8,128)} %fusion.3, bf16[1280,32]{0,1:T(8,128)(2,1)S(1)} %fusion.16, bf16[1,32,3584]{2,1,0:T(8,128)(2,1)S(1)} %copy-done.1, bf16[1280,3584]{1,0:T(8,128)(2,1)} %bitcast.58), kind=kOutput, calls=%fused_computation.17 | convolution fusion | flops 316537600 | bytes 27841536 | tf_op jit(solution)/shard_map/dot_general | solution.py:12
  212.5 0.7 stack_reshape.3
  213.2 39.7 %all-to-all-start.1 = ((f32[16,1,80]{2,1,0:T(1,128)}), f32[16,1,80]{2,1,0:T(1,128)S(1)}, u32[]{:S(2)}, u32[]{:S(2)}) async-start(f32[16,1,80]{2,1,0:T(1,128)} %stack_reshape.3), calls=%async_computation.1 | async-start | bytes 16384 | tf_op jit(solution)/shard_map/all_to_all | solution.py:93
  252.9 0.0 copy-done.4
  252.9 0.0 copy-done.5
  252.9 0.7 dynamic-slice
  253.6 5.6 %all-to-all-done.1 = f32[16,1,80]{2,1,0:T(1,128)S(1)} async-done(((f32[16,1,80]{2,1,0:T(1,128)}), f32[16,1,80]{2,1,0:T(1,128)S(1)}, u32[]{:S(2)}, u32[]{:S(2)}) %all-to-all-start.1) | async-done | bytes 5152 | tf_op jit(solution)/shard_map/all_to_all | solution.py:93
  259.2 0.5 broadcast.79
  259.7 0.7 reduce.7
  260.4 0.1 reshape.101
  260.4 6.1 %gather_fusion = f32[1024]{0:T(1024)S(1)} fusion(f32[1280]{0:T(1024)S(1)} %reshape.101, s32[1024]{0:T(1024)S(1)} %broadcast_clamp_fusion), kind=kCustom, calls=%fused_computation | custom fusion | bytes 12288 | tf_op jit(solution)/shard_map/gather | solution.py:94
  266.6 0.1 reshape.102
  266.8 0.6 fusion.34
  267.4 0.1 copy.69
  267.5 0.1 reshape.128
  267.6 7.6 %scatter_custom_fusion.1 = bf16[1280]{0:T(1024)(128)(2,1)S(1)} fusion(s32[1024]{0:T(1024)S(1)} %bitcast.73, bf16[1024]{0:T(1024)(128)(2,1)S(1)} %reshape.128, bf16[]{:T(256)} %constant.8.clone.1), kind=kCustom, calls=%fused_computation.47 | custom fusion | bytes 2562 | tf_op jit(solution)/shard_map/scatter | solution.py:43
  275.2 0.7 reshape.132
  275.9 3.5 all-to-all-start.2
  279.4 0.3 all-reduce.3.cloned.1.call-start
  279.6 0.0 copy-done.3
  279.7 2.1 fusion.38
  281.8 0.0 all-reduce.3.cloned.1.call-update
  281.8 3.8 %all-to-all-done.2 = bf16[16,1,80]{2,1,0:T(2,128)(2,1)S(1)} async-done(((bf16[16,1,80]{2,1,0:T(2,128)(2,1)}), bf16[16,1,80]{2,1,0:T(2,128)(2,1)S(1)}, u32[]{:S(2)}, u32[]{:S(2)}) %all-to-all-start.2) | async-done | bytes 2592 | tf_op jit(solution)/shard_map/all_to_all | solution.py:62
  285.7 0.1 reshape.107
  285.8 10.5 %multiply_convert_fusion = bf16[16,1,80,3584]{3,2,1,0:T(8,128)(2,1)} fusion(bf16[16,1,80,3584]{3,2,1,0:T(8,128)(2,1)} %all-to-all-done, f32[16,80]{1,0:T(8,128)S(1)} %bitcast.68), kind=kLoop, calls=%fused_computation.8 | loop fusion | flops 13762560 | bytes 18355200 | tf_op jit(solution)/shard_map/convert_element_type | solution.py:70
  296.3 8.0 %fusion.22 = f32[1,1024,32]{1,2,0:T(8,128)} fusion(bf16[1,1280,1024]{2,1,0:T(8,128)(2,1)S(1)} %copy-done, bf16[1280,3584]{1,0:T(8,128)(2,1)} %bitcast.66, bf16[1,32,3584]{2,1,0:T(8,128)(2,1)S(1)} %copy-done.1), kind=kOutput, calls=%fused_computation.26 | convolution fusion | flops 377561088 | bytes 12156928 | tf_op jit(solution)/shard_map/dot_general | solution.py:77
  304.3 10.6 %fusion.2 = bf16[1280,3584]{1,0:T(8,128)(2,1)} fusion(bf16[16,1,80,3584]{3,2,1,0:T(8,128)(2,1)} %all-to-all-done, f32[1280]{0:T(1024)S(1)} %reshape.107), kind=kLoop, calls=%fused_computation.7 | loop fusion | flops 13762560 | bytes 18355200 | tf_op jit(solution)/shard_map/convert_element_type | solution.py:70
  314.8 6.1 %fusion.8 = f32[1,32,3584]{2,1,0:T(8,128)} fusion(bf16[1280,32]{0,1:T(8,128)(2,1)S(1)} %fusion.16, bf16[1280,3584]{1,0:T(8,128)(2,1)} %fusion.2), kind=kOutput, calls=%fused_computation.15 | convolution fusion | flops 293715968 | bytes 9715712 | tf_op jit(solution)/shard_map/dot_general | solution.py:83
  320.9 52.4 %all-reduce.3.cloned.1.call-done = f32[16,3584]{1,0:T(8,128)} async-done(((f32[16,3584]{1,0:T(8,128)}), f32[16,3584]{1,0:T(8,128)}) %all-reduce.3.cloned.1.call-update) | async-done | bytes 229392
  373.3 2.2 constant_dynamic-slice_fusion
  (12 shorter events, 0.2 us)
Async XLA Ops:
  7.2 30.3 %copy-start = (bf16[1,1280,1024]{2,1,0:T(8,128)(2,1)S(1)}, bf16[1,1280,1024]{2,1,0:T(8,128)(2,1)}, u32[]{:S(2)}) copy-start(bf16[1,1280,1024]{2,1,0:T(8,128)(2,1)} %param.15) | copy-start | bytes 7864324
  29.9 7.6 %copy-start.2 = (bf16[1,1024,32]{1,2,0:T(8,128)(2,1)S(1)}, bf16[1,1024,32]{1,2,0:T(8,128)(2,1)}, u32[]{:S(2)}) copy-start(bf16[1,1024,32]{1,2,0:T(8,128)(2,1)} %param.13) | copy-start | bytes 196612
  29.9 171.9 %all-to-all-start = ((bf16[16,1,80,3584]{3,2,1,0:T(8,128)(2,1)}), bf16[16,1,80,3584]{3,2,1,0:T(8,128)(2,1)}, u32[]{:S(2)}, u32[]{:S(2)}) async-start(bf16[16,1,80,3584]{3,2,1,0:T(8,128)(2,1)} %bitcast.65), calls=%async_computation | async-start | bytes 18350080 | tf_op jit(solution)/shard_map/all_to_all | solution.py:61
  38.3 163.5 %copy-start.1 = (bf16[1,32,3584]{2,1,0:T(8,128)(2,1)S(1)}, bf16[1,32,3584]{2,1,0:T(8,128)(2,1)}, u32[]{:S(2)}) copy-start(bf16[1,32,3584]{2,1,0:T(8,128)(2,1)} %param.14) | copy-start | bytes 688132
  201.8 51.0 %copy-start.4 = (f32[128,8]{0,1:T(8,128)S(1)}, f32[128,8]{0,1:T(8,128)}, u32[]{:S(2)}) copy-start(f32[128,8]{0,1:T(8,128)} %param.10) | copy-start | bytes 12292
  201.8 51.1 %copy-start.5 = (u32[32]{0:T(128)S(1)}, u32[32]{0:T(128)}, u32[]{:S(2)}) copy-start(u32[32]{0:T(128)} %constant.31) | copy-start | bytes 388
  201.8 77.8 %copy-start.3 = (s32[128,8]{0,1:T(8,128)S(1)}, s32[128,8]{0,1:T(8,128)}, u32[]{:S(2)}) copy-start(s32[128,8]{0,1:T(8,128)} %param.11) | copy-start | bytes 12292
  213.2 46.0 %all-to-all-start.1 = ((f32[16,1,80]{2,1,0:T(1,128)}), f32[16,1,80]{2,1,0:T(1,128)S(1)}, u32[]{:S(2)}, u32[]{:S(2)}) async-start(f32[16,1,80]{2,1,0:T(1,128)} %stack_reshape.3), calls=%async_computation.1 | async-start | bytes 16384 | tf_op jit(solution)/shard_map/all_to_all | solution.py:93
  275.9 9.8 %all-to-all-start.2 = ((bf16[16,1,80]{2,1,0:T(2,128)(2,1)}), bf16[16,1,80]{2,1,0:T(2,128)(2,1)S(1)}, u32[]{:S(2)}, u32[]{:S(2)}) async-start(bf16[16,1,80]{2,1,0:T(2,128)(2,1)} %reshape.132), calls=%async_computation.2 | async-start | bytes 16384 | tf_op jit(solution)/shard_map/all_to_all | solution.py:62
  279.4 93.9 %all-reduce.3.cloned.1.call-start = ((), (), s32[]{:S(2)}) async-start(), calls=%async_computation.3 | async-start | bytes 458752
Sparse Core Ops, SparseCore 0:
  283.6 89.6 all-reduce.2
where the time goes:
time: 383 us; the launch traced here: 382 us
  waiting for transfers between devices  210 us (55%)
  starting transfers between devices  50.9 us (13%)
  matrix products  43.2 us (11%)
  local copies, waits for them, and re-layouts  36.3 us (9%)
  other arithmetic  27.8 us (7%)
  between operations  14.2 us (4%)
    all_to_all x1, waiting for transfers between devices, per_device(): lax.all_to_all(send_rows, 'expert', split_axis=0, concat_axis=0, tiled=True)  148 us
    unnamed x2, waiting for transfers between devices  52.4 us
    all_to_all x1, starting transfers between devices, per_device(): lax.all_to_all(dot_table, 'expert', split_axis=0, concat_axis=0, tiled=True)  39.7 us
    convert_element_type x2, other arithmetic, per_device(): scaled_output_gradient = (slot_scale.astype(jnp.float32)[:, None] * slot_...  21 us
    scatter x1, local copies, waits for them, and re-layouts, per_device(): jnp.zeros((experts * capacity, features), jnp.bfloat16).at[position]  15.7 us
    dot_general x1, matrix products, recompute_every_expert(): jnp.dot(hidden_activation, expert_down_matrix, preferred_element_type=jnp...  15.5 us
    dot_general x1, matrix products, recompute_every_expert(): jnp.dot(lowrank_hidden, second_factor, preferred_element_type=jnp.float32)  10.6 us
    dot_general x1, matrix products, per_device(): lax.dot_general(stored_hidden_rows[expert_number], backward_lowrank, (((0...  8.01 us
  transfers between devices with their start and end apart: 4, of which 4 were waited for; matrix products, arithmetic and copies ran while one was open for 14% of the time, Pallas kernels for 0%

commit v1 on v0

--- a/solution.py
+++ b/solution.py
@@ -1,9 +1,411 @@
+import functools
+
 import jax
 import jax.numpy as jnp
 from jax import lax
+from jax.experimental import pallas as pl
+from jax.experimental.pallas import tpu as pltpu
 from jax.sharding import PartitionSpec as P
 
+MESH = pl.DeviceIdType.MESH
 adapter_scale = 2.0
+
+NZ, NX, NC = 4, 2, 2
+PARTS = 4
+UP, DOWN, ACROSS, SIBLING = range(4)
+
+
+def gather_kernel(
+    grad_hbm, act_hbm, scores_ref, index_ref, weight_hbm, first_ref, second_ref, hidden_hbm,
+    csg_ref, first_out, second_out, router_out,
+    tokens, weight, hidden, act, expert_out, low, first_sum,
+    table_send, table_recv, dot_send, dot_recv, router_send, router_recv,
+    block_send_sem, block_recv_sem, table_send_sem, table_recv_sem,
+    dot_send_sem, dot_recv_sem, router_send_sem, router_recv_sem, local_sem,
+):
+    n = NZ * NX * NC
+    tok, feat = grad_hbm.shape
+    top = scores_ref.shape[1]
+    rank = second_ref.shape[0]
+    units = weight.shape[0]
+    cap = hidden.shape[0] // n
+    rows = tok // PARTS
+    me = lax.axis_index("expert")
+    z, x, c = me // 4, (me // 2) % 2, me % 2
+    f32, bf16 = jnp.float32, jnp.bfloat16
+
+    barrier = pltpu.get_barrier_semaphore()
+
+    def greet(i, _):
+        pl.semaphore_signal(
+            barrier, inc=1, device_id={"expert": (me + i) % n}, device_id_type=MESH
+        )
+        return 0
+
+    local = [
+        pltpu.make_async_copy(hidden_hbm, hidden, local_sem.at[0]),
+        pltpu.make_async_copy(weight_hbm, weight, local_sem.at[1]),
+        pltpu.make_async_copy(
+            grad_hbm,
+            tokens.at[z * 2 + x, pl.ds(pl.multiple_of(c * tok, tok), tok)],
+            local_sem.at[2],
+        ),
+        pltpu.make_async_copy(act_hbm, act, local_sem.at[3]),
+    ]
+    for copy in local:
+        copy.start()
+    lax.fori_loop(1, n, greet, 0)
+    pl.semaphore_wait(barrier, n - 1)
+
+    def piece(zz, xx, cc, part):
+        return tokens.at[
+            zz * 2 + xx, pl.ds(pl.multiple_of(cc * tok + part * rows, rows), rows)
+        ]
+
+    def move(kind, zz, xx, cc, part, source=None):
+        target = {
+            UP: me + 4, DOWN: me - 4, ACROSS: z * 4 + (1 - x) * 2 + c, SIBLING: z * 4 + x * 2 + 1 - c,
+        }[kind]
+        block = zz * 4 + xx * 2 + cc
+        place = piece(zz, xx, cc, part)
+        return pltpu.make_async_remote_copy(
+            src_ref=place if source is None else source,
+            dst_ref=place,
+            send_sem=block_send_sem.at[kind, block, part],
+            recv_sem=block_recv_sem.at[block, part],
+            device_id={"expert": target},
+            device_id_type=MESH,
+        )
+
+    def own(part, act_on):
+        source = grad_hbm.at[pl.ds(pl.multiple_of(part * rows, rows), rows)]
+        act_on(move(ACROSS, z, x, c, part, source))
+
+        @pl.when(z < NZ - 1)
+        def _():
+            act_on(move(UP, z, x, c, part, source))
+
+        @pl.when(z > 0)
+        def _():
+            act_on(move(DOWN, z, x, c, part, source))
+
+        act_on(move(SIBLING, z, x, c, part, source))
+
+    def start(copy):
+        copy.start()
+
+    def sent(copy):
+        copy.wait_send()
+
+    def own_start(part, _):
+        own(part, start)
+        return 0
+
+    lax.fori_loop(0, PARTS, own_start, 0)
+
+    scores = jnp.transpose(scores_ref[...])
+    index = jnp.transpose(index_ref[...])
+    score_sum = jnp.sum(scores, axis=0, keepdims=True)
+    weights = scores / score_sum
+    expert_row = lax.broadcasted_iota(jnp.int32, (n, tok), 0)
+    chosen = jnp.zeros((n, tok), f32)
+    scale = jnp.zeros((n, tok), f32)
+    for k in range(top):
+        hit = index[k : k + 1, :] == expert_row
+        chosen = jnp.where(hit, 1.0, chosen)
+        scale = jnp.where(hit, weights[k : k + 1, :], scale)
+    earlier = (
+        lax.broadcasted_iota(jnp.int32, (tok, tok), 0)
+        < lax.broadcasted_iota(jnp.int32, (tok, tok), 1)
+    ).astype(bf16)
+    slot = jnp.dot(chosen.astype(bf16), earlier, preferred_element_type=f32)
+    slot = jnp.where(chosen > 0.5, slot, -1.0)
+    scale = scale.astype(bf16).astype(f32)
+    pad = jnp.zeros((6, tok), f32)
+    for e in range(n):
+        table_send[e] = jnp.concatenate([slot[e : e + 1], scale[e : e + 1], pad], axis=0)
+    table_recv[me] = table_send[me]
+
+    def table_copy(to, source):
+        return pltpu.make_async_remote_copy(
+            src_ref=table_send.at[to],
+            dst_ref=table_recv.at[source],
+            send_sem=table_send_sem.at[to],
+            recv_sem=table_recv_sem.at[source],
+            device_id={"expert": to},
+            device_id_type=MESH,
+        )
+
+    def others(act_on):
+        def body(i, _):
+            act_on((me + i) % n)
+            return 0
+
+        lax.fori_loop(1, n, body, 0)
+
+    others(lambda to: table_copy(to, me).start())
+
+    local[0].wait()
+    low[...] = jnp.dot(hidden[...], first_ref[...], preferred_element_type=f32).astype(bf16)
+    local[1].wait()
+    first_sum[...] = jnp.zeros_like(first_sum)
+    second_out[...] = jnp.zeros_like(second_out)
+
+    tile = 512
+    tiles = feat // tile
+
+    def output_tile(i):
+        at = pl.ds(pl.multiple_of(i * tile, tile), tile)
+        expert_out[:, at] = (
+            jnp.dot(hidden[...], weight[:, at], preferred_element_type=f32)
+            + adapter_scale
+            * jnp.dot(low[...], second_ref[:, at], preferred_element_type=f32)
+        ).astype(bf16)
+
+    def dot_copy(to, source):
+        return pltpu.make_async_remote_copy(
+            src_ref=dot_send.at[to],
+            dst_ref=dot_recv.at[source],
+            send_sem=dot_send_sem.at[to],
+            recv_sem=dot_recv_sem.at[source],
+            device_id={"expert": to},
+            device_id_type=MESH,
+        )
+
+    def chip(zz, xx):
+        pair = zz * 2 + xx
+
+        def arrived(part, _):
+            move(SIBLING, zz, xx, 1 - c, part).wait_recv()
+            return 0
+
+        lax.fori_loop(0, PARTS, arrived, 0)
+        both = tokens[pair]
+        at = pl.ds(pl.multiple_of(pair * 2 * cap, 2 * cap), 2 * cap)
+        nt = (((1,), (1,)), ((), ()))
+        inner = lax.dot_general(expert_out[at, :], both, nt, preferred_element_type=f32)
+        back = lax.dot_general(second_ref[...], both, nt, preferred_element_type=f32)
+        t0, t1 = table_recv[2 * pair], table_recv[2 * pair + 1]
+        slots = jnp.concatenate([t0[0:1], jnp.where(t1[0:1] < 0.0, -1.0, t1[0:1] + cap)], axis=1)
+        scales = jnp.concatenate([t0[1:2], t1[1:2]], axis=1)
+        number = lax.broadcasted_iota(jnp.int32, (2 * cap, 2 * tok), 0).astype(f32)
+        match = number == slots
+        dots = jnp.sum(jnp.where(match, inner, 0.0), axis=0, keepdims=True)
+        for sub in range(2):
+            to = 2 * pair + sub
+            dot_send[to] = jnp.broadcast_to(dots[:, sub * tok : (sub + 1) * tok], (8, tok))
+
+            @pl.when(to != me)
+            def _():
+                dot_copy(to, me).start()
+
+            @pl.when(to == me)
+            def _():
+                dot_recv[to] = dot_send[to]
+
+        one_hot = match.astype(bf16)
+        back = (back * scales).astype(bf16)
+        back = lax.dot_general(back, one_hot, nt, preferred_element_type=f32).astype(bf16)
+        first_sum[...] += jnp.dot(back, hidden[at, :], preferred_element_type=f32)
+        spread = lax.dot_general(
+            low[at, :], one_hot, (((0,), (0,)), ((), ())), preferred_element_type=f32
+        )
+        spread = (adapter_scale * spread * scales).astype(bf16)
+        second_out[...] += jnp.dot(spread, both, preferred_element_type=f32)
+
+    def along(distance, part, act_on):
+        @pl.when(z >= distance)
+        def _():
+            zz = z - distance
+            act_on(zz, part, UP, z < NZ - 1)
+
+        @pl.when(z + distance < NZ)
+        def _():
+            zz = z + distance
+            act_on(zz, part, DOWN, z > 0)
+
+    def pass_on(zz, part, kind, more):
+        move(kind, zz, x, c, part).wait_recv()
+
+        @pl.when(more)
+        def _():
+            move(kind, zz, x, c, part).start()
+
+        move(ACROSS, zz, x, c, part).start()
+        move(SIBLING, zz, x, c, part).start()
+
+    def passed(zz, part, kind, more):
+        @pl.when(more)
+        def _():
+            move(kind, zz, x, c, part).wait_send()
+
+        move(ACROSS, zz, x, c, part).wait_send()
+        move(SIBLING, zz, x, c, part).wait_send()
+
+    def cross(zz, part, kind, more):
+        move(ACROSS, zz, 1 - x, c, part).wait_recv()
+        move(SIBLING, zz, 1 - x, c, part).start()
+
+    def crossed(zz, part, kind, more):
+        move(SIBLING, zz, 1 - x, c, part).wait_send()
+
+    def chips_of(phase, which):
+        side = which % 2
+        distance = jnp.where(which < 2, phase, phase + 1)
+        zz = jnp.where(side == 0, z - distance, z + distance)
+        xx = jnp.where(which < 2, 1 - x, x)
+        mine = (phase == 0) & (which == 1)
+        xx = jnp.where(mine, x, xx)
+        return zz, xx, (zz >= 0) & (zz < NZ)
+
+    def first_phase(part, _):
+        along(1, part, pass_on)
+        for j in range(2):
+            i = part * 2 + j
+
+            @pl.when(i < tiles)
+            def _():
+                output_tile(i)
+
+        cross(z, part, None, None)
+        return 0
+
+    lax.fori_loop(0, PARTS, first_phase, 0)
+    local[2].wait()
+    others(lambda source: table_copy(source, source).wait_recv())
+
+    def later(step, _):
+        phase, part = step // PARTS, step % PARTS
+
+        along(phase + 1, part, pass_on)
+        zz, xx, there = chips_of(phase - 1, part)
+
+        @pl.when(there)
+        def _():
+            chip(zz, xx)
+
+        along(phase, part, cross)
+        return 0
+
+    lax.fori_loop(PARTS, NZ * PARTS, later, 0)
+    for side in range(2):
+        zz, xx, there = chips_of(NZ - 1, side)
+
+        @pl.when(there)
+        def _():
+            chip(zz, xx)
+
+    first_out[...] = jnp.transpose(adapter_scale * first_sum[...])
+    local[3].wait()
+    others(lambda source: dot_copy(source, source).wait_recv())
+    dots = dot_recv[:, 0, :]
+    grads = []
+    for k in range(top):
+        hit = index[k : k + 1, :] == expert_row
+        grads.append(jnp.sum(jnp.where(hit, dots, 0.0), axis=0, keepdims=True))
+    weight_grad = jnp.concatenate(grads, axis=0)
+    mixed = jnp.sum(weights * weight_grad, axis=0, keepdims=True)
+    csg = (weight_grad - mixed) / score_sum
+    csg_ref[...] = jnp.transpose(csg)
+    logit = (csg * scores * (1.0 - scores)).astype(bf16).astype(f32)
+    router = jnp.zeros((n, tok), f32)
+    for k in range(top):
+        router = jnp.where(index[k : k + 1, :] == expert_row, logit[k : k + 1, :], router)
+    partial = jnp.dot(router.astype(bf16), act[...], preferred_element_type=f32)
+    for j in range(feat // 128):
+        router_send[:, j, :] = partial[:, j * 128 : (j + 1) * 128]
+    router_recv[me] = router_send[me]
+
+    def router_copy(to, source):
+        return pltpu.make_async_remote_copy(
+            src_ref=router_send.at[to],
+            dst_ref=router_recv.at[source],
+            send_sem=router_send_sem.at[to],
+            recv_sem=router_recv_sem.at[source],
+            device_id={"expert": to},
+            device_id_type=MESH,
+        )
+
+    others(lambda to: router_copy(to, me).start())
+
+    def drain(part, _):
+        own(part, sent)
+        crossed(z, part, None, None)
+        return 0
+
+    lax.fori_loop(0, PARTS, drain, 0)
+
+    def drain_later(step, _):
+        distance, part = step // PARTS, step % PARTS
+        along(distance, part, passed)
+        along(distance, part, crossed)
+        return 0
+
+    lax.fori_loop(PARTS, NZ * PARTS, drain_later, 0)
+    others(lambda to: table_copy(to, me).wait_send())
+    others(lambda to: dot_copy(to, me).wait_send())
+    others(lambda source: router_copy(source, source).wait_recv())
+    router_out[...] = jnp.sum(router_recv[...], axis=0)
+    others(lambda to: router_copy(to, me).wait_send())
+
+
+def per_device_gather(
+    output_gradient, activations, scores, chosen_expert_index,
+    frozen_down_weight, adapter_first, adapter_second, stored_hidden_rows,
+):
+    n = NZ * NX * NC
+    tok, feat = output_gradient.shape
+    units, rank = adapter_first.shape[1:]
+    slots = stored_hidden_rows.shape[1]
+    vmem = pl.BlockSpec(memory_space=pltpu.VMEM)
+    hbm = pl.BlockSpec(memory_space=pl.ANY)
+    f32, bf16 = jnp.float32, jnp.bfloat16
+    dma = pltpu.SemaphoreType.DMA
+    csg, first, second, router = pl.pallas_call(
+        gather_kernel,
+        out_shape=(
+            jax.ShapeDtypeStruct(scores.shape, f32),
+            jax.ShapeDtypeStruct((units, rank), f32),
+            jax.ShapeDtypeStruct((rank, feat), f32),
+            jax.ShapeDtypeStruct((feat // 128, 128), f32),
+        ),
+        in_specs=[hbm, hbm, vmem, vmem, hbm, vmem, vmem, hbm],
+        out_specs=(vmem,) * 4,
+        scratch_shapes=[
+            pltpu.VMEM((NZ * NX, NC * tok, feat), bf16),
+            pltpu.VMEM((units, feat), bf16),
+            pltpu.VMEM((slots, units), bf16),
+            pltpu.VMEM((tok, feat), bf16),
+            pltpu.VMEM((slots, feat), bf16),
+            pltpu.VMEM((slots, rank), bf16),
+            pltpu.VMEM((rank, units), f32),
+            pltpu.VMEM((n, 8, tok), f32),
+            pltpu.VMEM((n, 8, tok), f32),
+            pltpu.VMEM((n, 8, tok), f32),
+            pltpu.VMEM((n, 8, tok), f32),
+            pltpu.VMEM((n, feat // 128, 128), f32),
+            pltpu.VMEM((n, feat // 128, 128), f32),
+            dma((4, n, PARTS)),
+            dma((n, PARTS)),
+            dma((n,)),
+            dma((n,)),
+            dma((n,)),
+            dma((n,)),
+            dma((n,)),
+            dma((n,)),
+            dma((4,)),
+        ],
+        compiler_params=pltpu.CompilerParams(
+            collective_id=0, has_side_effects=True, vmem_limit_bytes=60 * 1024 * 1024
+        ),
+        cost_estimate=pl.CostEstimate(
+            flops=2 * slots * units * feat, bytes_accessed=2 * units * feat, transcendentals=0
+        ),
+    )(
+        output_gradient, activations, scores, chosen_expert_index,
+        frozen_down_weight[0], adapter_first[0], adapter_second[0], stored_hidden_rows[0],
+    )
+    return csg, first[None], second[None], router.reshape(1, feat)
 
 
 def recompute_every_expert(hidden_activation, lowrank_hidden, expert_down_matrix, second_factor):
@@ -124,8 +526,9 @@
         P("expert", None, None),
         P(("groups", "expert"), None, None),
     )
+    small = mesh.shape["expert"] == NZ * NX * NC
     return jax.shard_map(
-        per_device,
+        per_device_gather if small else per_device,
         mesh=mesh,
         in_specs=placed,
         out_specs=(

time: 383 us -> 116 us (0.30)
  waiting for transfers between devices: 210 us -> 0 us
  Pallas kernels: 0 us -> 104 us
  starting transfers between devices: 50.9 us -> 0 us
  matrix products: 43.2 us -> 0 us
  other arithmetic: 27.8 us -> 0 us
  local copies, waits for them, and re-layouts: 36.3 us -> 11 us
  between operations: 14.2 us -> 0.64 us
    all_to_all x3 -> x0, waiting for transfers between devices: 157 us -> none  [the longest x1 148 us: per_device(): lax.all_to_all(send_rows, 'expert', split_axis=0, concat_axis=0, tiled=True)]
    pallas_call x0 -> x1, Pallas kernels: none -> 104 us  [per_device_gather(): pl.pallas_call(gather_kernel, out_shape=(jax.ShapeDtypeStruct(scores.shap...]
    unnamed x2 -> x0, waiting for transfers between devices: 52.4 us -> none
    all_to_all x3 -> x0, starting transfers between devices: 50.7 us -> none  [the longest x1 39.7 us: per_device(): lax.all_to_all(dot_table, 'expert', split_axis=0, concat_axis=0, tiled=True)]
    dot_general x6 -> x0, matrix products: 43.2 us -> none  [the longest x1 15.5 us: recompute_every_expert(): jnp.dot(hidden_activation, expert_down_matrix, preferred_element_type=jnp...]
    scatter x2 -> x0, local copies, waits for them, and re-layouts: 23.3 us -> none  [the longest x1 15.7 us: per_device(): jnp.zeros((experts * capacity, features), jnp.bfloat16).at[position]]
    convert_element_type x6 -> x0, other arithmetic: 21.7 us -> none  [the longest x2 21 us: per_device(): scaled_output_gradient = (slot_scale.astype(jnp.float32)[:, None] * slot_...]
    unnamed x15 -> x7, local copies, waits for them, and re-layouts: 3.82 us -> 11 us
  transfers between devices with their start and end apart: 4 -> 0, of which waited for: 4 -> 0; matrix products, arithmetic and copies ran while one was open for 14% -> 0% of each run, Pallas kernels for 0% -> 0%
where the time goes in v1:
time: 116 us
  Pallas kernels  104 us (90%)
  local copies, waits for them, and re-layouts  11 us (9%)
    pallas_call x1, Pallas kernels, per_device_gather(): pl.pallas_call(gather_kernel, out_shape=(jax.ShapeDtypeStruct(scores.shap...  104 us
    unnamed x7, local copies, waits for them, and re-layouts  11 us

profile of v1, /device:TPU:0, one launch (start us, length us, event | category | flops | bytes accessed | tf_op | source)
XLA Modules:
  0.0 115.7 jit_solution(4132609992698896169)
XLA Ops:
  0.6 1.4 %copy.13.scores_ref = f32[128,8]{1,0:T(8,128)} copy(f32[128,8]{0,1:T(8,128)} %param.10) | data formatting | bytes 8192 | tf_op args[2]
  2.0 1.4 %copy.14.index_ref = s32[128,8]{1,0:T(8,128)} copy(s32[128,8]{0,1:T(8,128)} %param.11) | data formatting | bytes 8192 | tf_op args[3]
  3.5 1.7 %copy.12 = bf16[1,1024,32]{2,1,0:T(8,128)(2,1)} copy(bf16[1,1024,32]{1,2,0:T(8,128)(2,1)} %param.13) | data formatting | bytes 131072 | tf_op args[5]
  5.1 104.0 %shard_map.111 = (f32[128,8]{1,0:T(8,128)}, f32[1024,32]{1,0:T(8,128)}, f32[32,3584]{1,0:T(8,128)}, f32[28,128]{1,0:T(8,128)}) custom-call(bf16[128,3584]{1,0:T(8,128)(2,1)} %grad_hbm.1, bf16[128,3584]{1,0:T(8,128)(2,1)} %act_hbm.1, f32[128,8]{1,0:T(8,128)} %copy.13.scores_ref, s32[128,8]{1,0:T(8,128)} %copy.14.index_ref, bf16[1024,3584]{1,0:T(8,128)(2,1)} %bitcast.16, ...), custom_call_target="tpu_custom_call" | custom-call | flops 9395240960 | bytes 7340032 | tf_op jit(solution)/shard_map/pallas_call | solution.py:364
  109.2 1.5 %copy.15 = f32[128,8]{0,1:T(8,128)} copy(f32[128,8]{1,0:T(8,128)} %get-tuple-element.12) | data formatting | bytes 8192
  110.7 1.9 %copy.16 = f32[1,1024,32]{1,2,0:T(8,128)} copy(f32[1,1024,32]{2,1,0:T(8,128)} %bitcast.11) | data formatting | bytes 262144
  112.5 1.3 %copy.19 = f32[1,1,28,128]{3,1,2,0:T(1,128)} copy(f32[1,1,28,128]{3,2,1,0:T(8,128)} %bitcast.14) | data formatting | bytes 28672
  113.9 1.8 %copy.21 = f32[1,32,3584]{2,1,0:T(8,128)} copy(f32[1,32,3584]{2,1,0:T(8,128)} %bitcast.12) | data formatting | bytes 917504

commit v2 on v1

--- a/solution.py
+++ b/solution.py
@@ -11,7 +11,7 @@
 adapter_scale = 2.0
 
 NZ, NX, NC = 4, 2, 2
-PARTS = 4
+PARTS = 8
 UP, DOWN, ACROSS, SIBLING = range(4)
 
 
@@ -19,13 +19,13 @@
     grad_hbm, act_hbm, scores_ref, index_ref, weight_hbm, first_ref, second_ref, hidden_hbm,
     csg_ref, first_out, second_out, router_out,
     tokens, weight, hidden, act, expert_out, low, first_sum,
-    table_send, table_recv, dot_send, dot_recv, router_send, router_recv,
+    table_send, table_recv, dot_send, dot_recv, router_sum, router_send, router_recv,
     block_send_sem, block_recv_sem, table_send_sem, table_recv_sem,
     dot_send_sem, dot_recv_sem, router_send_sem, router_recv_sem, local_sem,
 ):
     n = NZ * NX * NC
     tok, feat = grad_hbm.shape
-    top = scores_ref.shape[1]
+    top = scores_ref.shape[0]
     rank = second_ref.shape[0]
     units = weight.shape[0]
     cap = hidden.shape[0] // n
@@ -103,8 +103,8 @@
 
     lax.fori_loop(0, PARTS, own_start, 0)
 
-    scores = jnp.transpose(scores_ref[...])
-    index = jnp.transpose(index_ref[...])
+    scores = scores_ref[...]
+    index = index_ref[...]
     score_sum = jnp.sum(scores, axis=0, keepdims=True)
     weights = scores / score_sum
     expert_row = lax.broadcasted_iota(jnp.int32, (n, tok), 0)
@@ -146,9 +146,12 @@
     others(lambda to: table_copy(to, me).start())
 
     local[0].wait()
-    low[...] = jnp.dot(hidden[...], first_ref[...], preferred_element_type=f32).astype(bf16)
+    low[...] = lax.dot_general(
+        hidden[...], first_ref[...], (((1,), (1,)), ((), ())), preferred_element_type=f32
+    ).astype(bf16)
     local[1].wait()
     first_sum[...] = jnp.zeros_like(first_sum)
+    router_sum[...] = jnp.zeros_like(router_sum)
     second_out[...] = jnp.zeros_like(second_out)
 
     tile = 512
@@ -224,30 +227,47 @@
             zz = z + distance
             act_on(zz, part, DOWN, z > 0)
 
-    def pass_on(zz, part, kind, more):
-        move(kind, zz, x, c, part).wait_recv()
+    def by_line(zz, part):
+        return part >= jnp.where((zz == 0) | (zz == 3), 6, 7)
+
+    def pass_on(zz, part, kind, more, act_on=start):
+        if act_on is start:
+            move(kind, zz, x, c, part).wait_recv()
 
         @pl.when(more)
         def _():
-            move(kind, zz, x, c, part).start()
-
-        move(ACROSS, zz, x, c, part).start()
-        move(SIBLING, zz, x, c, part).start()
-
-    def passed(zz, part, kind, more):
-        @pl.when(more)
-        def _():
-            move(kind, zz, x, c, part).wait_send()
-
-        move(ACROSS, zz, x, c, part).wait_send()
-        move(SIBLING, zz, x, c, part).wait_send()
-
-    def cross(zz, part, kind, more):
-        move(ACROSS, zz, 1 - x, c, part).wait_recv()
-        move(SIBLING, zz, 1 - x, c, part).start()
-
-    def crossed(zz, part, kind, more):
-        move(SIBLING, zz, 1 - x, c, part).wait_send()
+            act_on(move(kind, zz, x, c, part))
+
+        @pl.when(jnp.logical_not(by_line(zz, part)))
+        def _():
+            act_on(move(ACROSS, zz, x, c, part))
+
+        act_on(move(SIBLING, zz, x, c, part))
+
+    def cross(zz, part, kind, more, act_on=start):
+        if act_on is start:
+            move(ACROSS, zz, 1 - x, c, part).wait_recv()
+
+        @pl.when(more & by_line(zz, part))
+        def _():
+            act_on(move(kind, zz, 1 - x, c, part))
+
+        act_on(move(SIBLING, zz, 1 - x, c, part))
+
+    def cross_own(part, act_on=start):
+        if act_on is start:
+            move(ACROSS, z, 1 - x, c, part).wait_recv()
+        inject = by_line(z, part)
+
+        @pl.when(inject & (z < NZ - 1))
+        def _():
+            act_on(move(UP, z, 1 - x, c, part))
+
+        @pl.when(inject & (z > 0))
+        def _():
+            act_on(move(DOWN, z, 1 - x, c, part))
+
+        act_on(move(SIBLING, z, 1 - x, c, part))
 
     def chips_of(phase, which):
         side = which % 2
@@ -267,7 +287,7 @@
             def _():
                 output_tile(i)
 
-        cross(z, part, None, None)
+        cross_own(part)
         return 0
 
     lax.fori_loop(0, PARTS, first_phase, 0)
@@ -280,7 +300,7 @@
         along(phase + 1, part, pass_on)
         zz, xx, there = chips_of(phase - 1, part)
 
-        @pl.when(there)
+        @pl.when(there & (part < 4))
         def _():
             chip(zz, xx)
 
@@ -295,7 +315,7 @@
         def _():
             chip(zz, xx)
 
-    first_out[...] = jnp.transpose(adapter_scale * first_sum[...])
+    first_out[...] = adapter_scale * first_sum[...]
     local[3].wait()
     others(lambda source: dot_copy(source, source).wait_recv())
     dots = dot_recv[:, 0, :]
@@ -306,14 +326,15 @@
     weight_grad = jnp.concatenate(grads, axis=0)
     mixed = jnp.sum(weights * weight_grad, axis=0, keepdims=True)
     csg = (weight_grad - mixed) / score_sum
-    csg_ref[...] = jnp.transpose(csg)
+    csg_ref[...] = csg
     logit = (csg * scores * (1.0 - scores)).astype(bf16).astype(f32)
     router = jnp.zeros((n, tok), f32)
     for k in range(top):
         router = jnp.where(index[k : k + 1, :] == expert_row, logit[k : k + 1, :], router)
     partial = jnp.dot(router.astype(bf16), act[...], preferred_element_type=f32)
     for j in range(feat // 128):
-        router_send[:, j, :] = partial[:, j * 128 : (j + 1) * 128]
+        router_sum[:, j, :] = partial[:, j * 128 : (j + 1) * 128]
+    router_send[...] = router_sum[...].astype(bf16)
     router_recv[me] = router_send[me]
 
     def router_copy(to, source):
@@ -330,23 +351,32 @@
 
     def drain(part, _):
         own(part, sent)
-        crossed(z, part, None, None)
+        cross_own(part, sent)
         return 0
 
     lax.fori_loop(0, PARTS, drain, 0)
 
     def drain_later(step, _):
         distance, part = step // PARTS, step % PARTS
-        along(distance, part, passed)
-        along(distance, part, crossed)
+        along(distance, part, functools.partial(pass_on, act_on=sent))
+        along(distance, part, functools.partial(cross, act_on=sent))
         return 0
 
     lax.fori_loop(PARTS, NZ * PARTS, drain_later, 0)
     others(lambda to: table_copy(to, me).wait_send())
     others(lambda to: dot_copy(to, me).wait_send())
     others(lambda source: router_copy(source, source).wait_recv())
-    router_out[...] = jnp.sum(router_recv[...], axis=0)
+    total = jnp.sum(router_recv[...].astype(f32), axis=0)
+    router_out[...] = total[: feat // 128]
     others(lambda to: router_copy(to, me).wait_send())
+
+
+def hand_over(csg_ref, first_ref, second_ref, router_ref, csg_out, first_out, second_out, router_out):
+    csg_out[...] = csg_ref[...]
+    first_out[...] = first_ref[...]
+    second_out[...] = second_ref[...]
+    for j in range(router_ref.shape[0]):
+        router_out[:, j * 128 : (j + 1) * 128] = router_ref[j : j + 1, :]
 
 
 def per_device_gather(
@@ -360,12 +390,13 @@
     vmem = pl.BlockSpec(memory_space=pltpu.VMEM)
     hbm = pl.BlockSpec(memory_space=pl.ANY)
     f32, bf16 = jnp.float32, jnp.bfloat16
+    padded = -(-feat // 2048) * 16
     dma = pltpu.SemaphoreType.DMA
     csg, first, second, router = pl.pallas_call(
         gather_kernel,
         out_shape=(
-            jax.ShapeDtypeStruct(scores.shape, f32),
-            jax.ShapeDtypeStruct((units, rank), f32),
+            jax.ShapeDtypeStruct(scores.shape[::-1], f32),
+            jax.ShapeDtypeStruct((rank, units), f32),
             jax.ShapeDtypeStruct((rank, feat), f32),
             jax.ShapeDtypeStruct((feat // 128, 128), f32),
         ),
@@ -383,8 +414,9 @@
             pltpu.VMEM((n, 8, tok), f32),
             pltpu.VMEM((n, 8, tok), f32),
             pltpu.VMEM((n, 8, tok), f32),
-            pltpu.VMEM((n, feat // 128, 128), f32),
-            pltpu.VMEM((n, feat // 128, 128), f32),
+            pltpu.VMEM((n, padded, 128), f32),
+            pltpu.VMEM((n, padded, 128), bf16),
+            pltpu.VMEM((n, padded, 128), bf16),
             dma((4, n, PARTS)),
             dma((n, PARTS)),
             dma((n,)),
@@ -402,10 +434,21 @@
             flops=2 * slots * units * feat, bytes_accessed=2 * units * feat, transcendentals=0
         ),
     )(
-        output_gradient, activations, scores, chosen_expert_index,
-        frozen_down_weight[0], adapter_first[0], adapter_second[0], stored_hidden_rows[0],
-    )
-    return csg, first[None], second[None], router.reshape(1, feat)
+        output_gradient, activations, scores.T, chosen_expert_index.T,
+        frozen_down_weight[0], adapter_first[0].T, adapter_second[0], stored_hidden_rows[0],
+    )
+    csg, first, second, router = pl.pallas_call(
+        hand_over,
+        out_shape=(
+            jax.ShapeDtypeStruct(csg.shape, f32),
+            jax.ShapeDtypeStruct(first.shape, f32),
+            jax.ShapeDtypeStruct(second.shape, f32),
+            jax.ShapeDtypeStruct((1, feat), f32),
+        ),
+        in_specs=[vmem] * 4,
+        out_specs=(vmem,) * 4,
+    )(csg, first, second, router)
+    return csg.T, first.T[None], second[None], router
 
 
 def recompute_every_expert(hidden_activation, lowrank_hidden, expert_down_matrix, second_factor):

time: 116 us -> 103 us (0.89)
  local copies, waits for them, and re-layouts: 11 us -> 0 us
  Pallas kernels: 104 us -> 102 us
    unnamed x7 -> x0, local copies, waits for them, and re-layouts: 11 us -> none
    pallas_call x1, Pallas kernels: 104 us -> 101 us  [per_device_gather(): pl.pallas_call(gather_kernel, out_shape=(jax.ShapeDtypeStruct(scores.shap...]
    pallas_call x0 -> x1, Pallas kernels: none -> 1.93 us  [per_device_gather(): pl.pallas_call(hand_over, out_shape=(jax.ShapeDtypeStruct(csg.shape, f32)...]
where the time goes in v2:
time: 103 us
  Pallas kernels  102 us (99%)
    pallas_call x1, Pallas kernels, per_device_gather(): pl.pallas_call(gather_kernel, out_shape=(jax.ShapeDtypeStruct(scores.shap...  101 us

profile of v2, /device:TPU:0, one launch (start us, length us, event | category | flops | bytes accessed | tf_op | source)
XLA Modules:
  0.0 103.1 jit_solution(3677937004957885783)
XLA Ops:
  0.6 100.6 %shard_map.111 = (f32[8,128]{1,0:T(8,128)}, f32[32,1024]{1,0:T(8,128)}, f32[32,3584]{1,0:T(8,128)}, f32[28,128]{1,0:T(8,128)}) custom-call(bf16[128,3584]{1,0:T(8,128)(2,1)} %grad_hbm.1, bf16[128,3584]{1,0:T(8,128)(2,1)} %act_hbm.1, f32[8,128]{1,0:T(8,128)} %bitcast.19, s32[8,128]{1,0:T(8,128)} %bitcast.20, bf16[1024,3584]{1,0:T(8,128)(2,1)} %bitcast.13, ...), custom_call_target="tpu_custom_call" | custom-call | flops 9395240960 | bytes 7340032 | tf_op jit(solution)/shard_map/pallas_call | solution.py:395
  101.2 1.9 %shard_map.112 = (f32[8,128]{1,0:T(8,128)}, f32[32,1024]{1,0:T(8,128)}, f32[32,3584]{1,0:T(8,128)}, f32[1,3584]{1,0:T(1,128)}) custom-call(f32[8,128]{1,0:T(8,128)} %get-tuple-element.12.csg_ref, f32[32,1024]{1,0:T(8,128)} %get-tuple-element.13.first_ref, f32[32,3584]{1,0:T(8,128)} %get-tuple-element.14.second_ref, f32[28,128]{1,0:T(8,128)} %get-tuple-element.15.router_ref), custom_call_target="tpu_custom_call" | custom-call | tf_op jit(solution)/shard_map/pallas_call | solution.py:440

commit v3 on v2

--- a/solution.py
+++ b/solution.py
@@ -228,7 +228,7 @@
             act_on(zz, part, DOWN, z > 0)
 
     def by_line(zz, part):
-        return part >= jnp.where((zz == 0) | (zz == 3), 6, 7)
+        return part < jnp.where((zz == 0) | (zz == 3), 2, 1)
 
     def pass_on(zz, part, kind, more, act_on=start):
         if act_on is start:

time: 103 us -> 103 us (level)
  no operation moved by 1% of the time
where the time goes in v3:
time: 103 us
  Pallas kernels  102 us (99%)
    pallas_call x1, Pallas kernels, per_device_gather(): pl.pallas_call(gather_kernel, out_shape=(jax.ShapeDtypeStruct(scores.shap...  100 us

profile of v3, /device:TPU:0, one launch (start us, length us, event | category | flops | bytes accessed | tf_op | source)
XLA Modules:
  0.0 102.6 jit_solution(12675370678536059313)
XLA Ops:
  0.6 100.0 %shard_map.111 = (f32[8,128]{1,0:T(8,128)}, f32[32,1024]{1,0:T(8,128)}, f32[32,3584]{1,0:T(8,128)}, f32[28,128]{1,0:T(8,128)}) custom-call(bf16[128,3584]{1,0:T(8,128)(2,1)} %grad_hbm.1, bf16[128,3584]{1,0:T(8,128)(2,1)} %act_hbm.1, f32[8,128]{1,0:T(8,128)} %bitcast.19, s32[8,128]{1,0:T(8,128)} %bitcast.20, bf16[1024,3584]{1,0:T(8,128)(2,1)} %bitcast.13, ...), custom_call_target="tpu_custom_call" | custom-call | flops 9395240960 | bytes 7340032 | tf_op jit(solution)/shard_map/pallas_call | solution.py:395
  100.6 1.9 %shard_map.112 = (f32[8,128]{1,0:T(8,128)}, f32[32,1024]{1,0:T(8,128)}, f32[32,3584]{1,0:T(8,128)}, f32[1,3584]{1,0:T(1,128)}) custom-call(f32[8,128]{1,0:T(8,128)} %get-tuple-element.12.csg_ref, f32[32,1024]{1,0:T(8,128)} %get-tuple-element.13.first_ref, f32[32,3584]{1,0:T(8,128)} %get-tuple-element.14.second_ref, f32[28,128]{1,0:T(8,128)} %get-tuple-element.15.router_ref), custom_call_target="tpu_custom_call" | custom-call | tf_op jit(solution)/shard_map/pallas_call | solution.py:440
